TPU v7x, 32 devices: a whole 2x2x4 slice. The times are simulated.
32 devices in a mesh: doc: 2 (over y), seq: 4 (over z), sub: 4 (over x, core).
Axes of the slice: x: 2, y: 2, z: 4, core: 2. Of those that a mesh axis runs over, the one named last changes fastest.
Arguments:
- queries: bfloat16 [16384, 512], P(('doc', 'seq', 'sub')), parts along dimension 0, may hold values from -18 to 18
- keys: bfloat16 [16384, 512], P(('doc', 'seq', 'sub')), parts along dimension 0, may hold values from -18 to 18
- values: bfloat16 [16384, 512], P(('doc', 'seq', 'sub')), parts along dimension 0, may hold values from -18 to 18
- seg_lengths: int32 [512], P('doc'), parts along dimension 0, may hold values from 1 to 64, 8192 in all
Outputs:
- attended: bfloat16 [16384, 512], P(('doc', 'seq', 'sub')), parts along dimension 0
There are 2 independent parts, one for each index of `doc`. A program takes and returns all parts, laid end to end along the dimension named above; each array names one. Nothing has to cross between parts.
Inputs may be any that keep to these rules, and one draw needn't show every extreme that they name: `seg_lengths`: the 256 segments cover all 8192 tokens in order; the longest has exactly 64 tokens.
All inputs are finite; a program needn't handle non-finite values.
Results may differ from a plain program's by a relative error of at most 0.012.
Values may be sent and summed in bfloat16 or wider, within the bound.
A program may use at most 64 MiB of HBM per device.

v0:
```python
import math
import jax
import jax.numpy as jnp
from jax import lax
from jax.sharding import PartitionSpec as P

H = 8
HD = 64
M = 256
ITERS = 3
HIGH_PRECISION = lax.Precision.HIGHEST


def row_softmax(score_matrix):
    row_top = jnp.max(score_matrix, axis=-1, keepdims=True)
    exponentials = jnp.exp(score_matrix - row_top)
    return exponentials / jnp.sum(exponentials, axis=-1, keepdims=True)


def iterative_pseudo_inverse(kernel):
    absval = jnp.abs(kernel)
    row_most = jnp.max(jnp.sum(absval, axis=2), axis=1)
    col_most = jnp.max(jnp.sum(absval, axis=1), axis=1)
    iterate = jnp.transpose(kernel, (0, 2, 1)) / (row_most * col_most)[:, None, None]
    identity = jnp.eye(kernel.shape[1], dtype=jnp.float32)[None]
    for sweep in range(ITERS):
        product = jnp.einsum("hij,hjk->hik", kernel, iterate, precision=HIGH_PRECISION)
        nested = jnp.einsum(
            "hij,hjk->hik", product, 7.0 * identity - product, precision=HIGH_PRECISION
        )
        nested = jnp.einsum(
            "hij,hjk->hik", product, 15.0 * identity - nested, precision=HIGH_PRECISION
        )
        iterate = 0.25 * jnp.einsum(
            "hij,hjk->hik", iterate, 13.0 * identity - nested, precision=HIGH_PRECISION
        )
    return iterate


def solve_mixing(query_head_rows, key_head_rows, landmark_values, score_scaling):
    landmark_kernel = row_softmax(
        jnp.einsum(
            "raj,taj->art", query_head_rows, key_head_rows, preferred_element_type=jnp.float32
        )
        * score_scaling
    )
    approx_inverse = iterative_pseudo_inverse(landmark_kernel)
    return jnp.einsum(
        "gux,gxr->gur", approx_inverse, landmark_values, precision=HIGH_PRECISION
    ).astype(jnp.bfloat16)


def shards(queries, keys, values, seg_lengths):
    row_count = queries.shape[0]
    width = queries.shape[1]
    score_scaling = 1.0 / math.sqrt(HD)
    shard = lax.axis_index("seq") * lax.axis_size("sub") + lax.axis_index("sub")
    positions = shard * row_count + lax.iota(jnp.int32, row_count)
    seg_ends = jnp.cumsum(seg_lengths)
    seg_begins = seg_ends - seg_lengths
    member = (
        (positions[:, None] >= seg_begins[None, :]) & (positions[:, None] < seg_ends[None, :])
    ).astype(jnp.bfloat16)
    counts = seg_lengths.astype(jnp.float32)
    contract = (((0,), (0,)), ((), ()))
    q_part = lax.dot_general(member, queries, contract, preferred_element_type=jnp.float32)
    k_part = lax.dot_general(member, keys, contract, preferred_element_type=jnp.float32)
    q_sums, k_sums = lax.psum((q_part, k_part), ("seq", "sub"))
    query_landmarks = (q_sums / counts[:, None]).astype(jnp.bfloat16)
    key_landmarks = (k_sums / counts[:, None]).astype(jnp.bfloat16)
    query_head_rows = query_landmarks.reshape(M, H, HD)
    key_head_rows = key_landmarks.reshape(M, H, HD)
    value_head_rows = values.reshape(row_count, H, HD)
    score_matrix = (
        jnp.einsum(
            "czy,rzy->zcr",
            query_head_rows,
            keys.reshape(row_count, H, HD),
            preferred_element_type=jnp.float32,
        )
        * score_scaling
    )
    row_top = lax.pmax(jnp.max(score_matrix, axis=2), ("seq", "sub"))
    exponentials = jnp.exp(score_matrix - row_top[:, :, None])
    total = jnp.sum(exponentials, axis=2)
    numer = jnp.einsum(
        "ijv,vib->ijb",
        exponentials,
        value_head_rows,
        precision=HIGH_PRECISION,
        preferred_element_type=jnp.float32,
    )
    total, numer = lax.psum((total, numer), ("seq", "sub"))
    landmark_values = numer / total[:, :, None]
    mixing_matrix = solve_mixing(query_head_rows, key_head_rows, landmark_values, score_scaling)
    scores_one = (
        jnp.einsum(
            "fxp,oxp->fxo",
            queries.reshape(row_count, H, HD),
            key_head_rows,
            preferred_element_type=jnp.float32,
        )
        * score_scaling
    )
    weight_matrix = row_softmax(scores_one).astype(jnp.bfloat16)
    attended = jnp.einsum(
        "ugf,gfa->uga", weight_matrix, mixing_matrix, preferred_element_type=jnp.float32
    )
    return attended.reshape(row_count, width).astype(jnp.bfloat16)


def solution(mesh):
    placed = (
        P(("doc", "seq", "sub"), None),
        P(("doc", "seq", "sub"), None),
        P(("doc", "seq", "sub"), None),
        P("doc"),
    )
    return jax.shard_map(
        shards,
        mesh=mesh,
        in_specs=placed,
        out_specs=P(("doc", "seq", "sub"), None),
        check_vma=False,
    )
```

profile of v0, /device:TPU:0, one launch (start us, length us, event | category | flops | bytes accessed | tf_op | source)
XLA Modules:
  0.0 319.6 jit_solution(4167720343065813831)
XLA Ops:
  8.7 2.3 fusion.59
  13.8 90.1 %all-reduce.4.cloned.1.call-done = f32[256,512]{1,0:T(8,128)} async-done(((f32[256,512]{1,0:T(8,128)}), f32[256,512]{1,0:T(8,128)}) %all-reduce.4.cloned.1.call-update) | async-done | bytes 524304 | tf_op jit(solution)/shard_map/psum | solution.py:68
  105.3 2.7 multiply_reduce_fusion
  107.9 32.4 %pmax.7 = f32[8,256]{1,0:T(8,128)S(1)} all-reduce(f32[8,256]{1,0:T(8,128)S(1)} %get-tuple-element.12), channel_id=1, replica_groups=mesh['doc'=2,'seq'=4,'sub'=4] {'seq','sub'}, use_global_device_ids=true, to_apply=%region_11.12 | all-reduce | flops 2048 | bytes 16384 | tf_op jit(solution)/shard_map/pmax | solution.py:83
  140.4 5.8 %fusion.6 = f32[8,256,64]{1,2,0:T(8,128)} fusion(bf16[512,8,64]{0,2,1:T(8,128)(2,1)S(1)} %bitcast.54, f32[8,256,512]{2,1,0:T(8,128)} %get-tuple-element.13, f32[8,256]{1,0:T(8,128)S(1)} %pmax.7), kind=kOutput, calls=%fused_computation.11 | convolution fusion | flops 807403520 | bytes 5251072 | tf_op jit(solution)/shard_map/ijv,vib->ijb/dot_general | solution.py:86
  146.2 3.1 fusion.5
  149.4 30.5 %psum.31 = f32[8,256]{1,0:T(8,128)S(1)} all-reduce(f32[8,256]{1,0:T(8,128)S(1)} %fusion.5), channel_id=1, replica_groups=mesh['doc'=2,'seq'=4,'sub'=4] {'seq','sub'}, use_global_device_ids=true, to_apply=%region_14.15 | all-reduce | flops 2048 | bytes 16384 | tf_op jit(solution)/shard_map/psum | solution.py:93
  179.9 57.3 %all-reduce.6.cloned.1.call-done = (f32[256,512]{1,0:T(8,128)}, f32[8,256,64]{1,2,0:T(8,128)}) async-done(((f32[256,512]{1,0:T(8,128)}, f32[8,256,64]{1,2,0:T(8,128)}), (f32[256,512]{1,0:T(8,128)}, f32[8,256,64]{1,2,0:T(8,128)})) %all-reduce.6.cloned.1.call-update) | async-done | bytes 1048592 | tf_op jit(solution)/shard_map/psum | solution.py:68
  243.8 2.9 copy.29
  246.7 8.1 %online-softmax = f32[8,256,256]{2,1,0:T(8,128)} custom-call(f32[8,256,256]{2,1,0:T(8,128)} %convolution_multiply_fusion, f32[8,256,256]{2,1,0:T(8,128)} %copy.29), custom_call_target="tpu_custom_call" | custom-call | tf_op online-softmax
  254.9 4.6 %fusion.13 = f32[8,256,256]{2,1,0:T(8,128)S(1)} fusion(f32[8,256,256]{2,1,0:T(8,128)} %online-softmax, f32[256,256]{1,0:T(8,128)S(1)} %fusion.61), kind=kOutput, calls=%fused_computation.16 | convolution fusion | flops 1611137024 | bytes 4456448 | tf_op jit(solution)/shard_map/hij,hjk->hik/dot_general | solution.py:28
  259.4 2.3 fusion.30
  261.7 5.0 %fusion.33 = f32[8,256,256]{2,1,0:T(8,128)} fusion(f32[8,256,256]{1,2,0:T(8,128)S(1)} %copy-done.5, f32[8,256,256]{2,1,0:T(8,128)S(1)} %fusion.30, f32[256,256]{1,0:T(8,128)S(1)} %fusion.63), kind=kOutput, calls=%fused_computation.39 | convolution fusion | flops 1611661312 | bytes 6553600 | tf_op jit(solution)/shard_map/hij,hjk->hik/dot_general | solution.py:34
  266.7 8.1 %online-softmax.1 = f32[8,256,256]{2,1,0:T(8,128)} custom-call(f32[8,256,256]{2,1,0:T(8,128)} %convolution_multiply_fusion, f32[8,256,256]{2,1,0:T(8,128)} %fusion.33), custom_call_target="tpu_custom_call" | custom-call | tf_op online-softmax
  274.8 4.6 %fusion.11 = f32[8,256,256]{2,1,0:T(8,128)S(1)} fusion(f32[8,256,256]{2,1,0:T(8,128)} %online-softmax.1, f32[256,256]{1,0:T(8,128)S(1)} %fusion.61), kind=kOutput, calls=%fused_computation.14 | convolution fusion | flops 1611137024 | bytes 4456448 | tf_op jit(solution)/shard_map/hij,hjk->hik/dot_general | solution.py:28
  279.4 2.3 fusion.26
  281.7 3.5 %fusion.36 = f32[8,256,256]{2,1,0:T(8,128)} fusion(f32[8,256,256]{2,1,0:T(8,128)S(1)} %copy-done.4, f32[8,256,256]{2,1,0:T(8,128)S(1)} %fusion.26, f32[256,256]{1,0:T(8,128)S(1)} %fusion.63), kind=kOutput, calls=%fused_computation.40 | convolution fusion | flops 1611661312 | bytes 6553600 | tf_op jit(solution)/shard_map/hij,hjk->hik/dot_general | solution.py:34
  285.2 8.1 %online-softmax.2 = f32[8,256,256]{2,1,0:T(8,128)} custom-call(f32[8,256,256]{2,1,0:T(8,128)} %convolution_multiply_fusion, f32[8,256,256]{2,1,0:T(8,128)} %fusion.36), custom_call_target="tpu_custom_call" | custom-call | tf_op online-softmax
  293.3 4.6 %fusion.9 = f32[8,256,256]{2,1,0:T(8,128)S(1)} fusion(f32[8,256,256]{2,1,0:T(8,128)} %online-softmax.2, f32[256,256]{1,0:T(8,128)S(1)} %fusion.61), kind=kOutput, calls=%fused_computation.12 | convolution fusion | flops 1611137024 | bytes 4456448 | tf_op jit(solution)/shard_map/hij,hjk->hik/dot_general | solution.py:28
  297.9 2.3 fusion.22
  300.2 2.2 fusion.20
  302.4 3.4 %fusion.76 = (f32[512,8]{0,1:T(8,128)S(1)}, f32[512,8,256]{0,2,1:T(8,128)}) fusion(bf16[256,8,64]{0,2,1:T(8,128)(2,1)S(1)} %bitcast.53, bf16[512,8,64]{0,2,1:T(8,128)(2,1)S(1)} %bitcast.56), kind=kOutput, calls=%fused_computation.83 | convolution fusion | flops 137363712 | bytes 4997120 | tf_op jit(solution)/shard_map/sub | solution.py:16
  305.8 3.2 %fusion.40 = bf16[8,256,64]{1,2,0:T(8,128)(2,1)S(1)} fusion(f32[8,256,256]{2,1,0:T(8,128)S(1)} %fusion.20, f32[8,256,64]{1,2,0:T(8,128)} %get-tuple-element.8, f32[8,256]{1,0:T(8,128)S(1)} %psum.31), kind=kOutput, calls=%fused_computation.43 | convolution fusion | flops 403439616 | bytes 2891776 | tf_op jit(solution)/shard_map/gux,gxr->gur/dot_general | solution.py:48
  309.1 2.7 fusion.39
  (49 shorter events, 14.0 us)
Async XLA Ops:
  6.5 4.6 %copy-start.6 = (bf16[512,512]{1,0:T(8,128)(2,1)S(1)}, bf16[512,512]{1,0:T(8,128)(2,1)}, u32[]{:S(2)}) copy-start(bf16[512,512]{1,0:T(8,128)(2,1)} %param.4) | copy-start | bytes 1572868
  6.5 5.6 %copy-start.8 = (bf16[512,512]{1,0:T(8,128)(2,1)S(1)}, bf16[512,512]{1,0:T(8,128)(2,1)}, u32[]{:S(2)}) copy-start(bf16[512,512]{1,0:T(8,128)(2,1)} %param.6) | copy-start | bytes 1572868
  6.5 5.8 %copy-start.7 = (bf16[512,512]{1,0:T(8,128)(2,1)S(1)}, bf16[512,512]{1,0:T(8,128)(2,1)}, u32[]{:S(2)}) copy-start(bf16[512,512]{1,0:T(8,128)(2,1)} %param.5) | copy-start | bytes 1572868
  6.5 97.4 %all-reduce.4.cloned.1.call-start = ((), (), s32[]{:S(2)}) async-start(), calls=%async_computation | async-start | bytes 1048576 | tf_op jit(solution)/shard_map/psum | solution.py:68
  11.0 226.1 %all-reduce.6.cloned.1.call-start = ((), (), s32[]{:S(2)}) async-start(), calls=%async_computation.1 | async-start | bytes 2097152 | tf_op jit(solution)/shard_map/psum | solution.py:68
  254.8 4.6 %copy-start.1 = (f32[8,256,256]{2,1,0:T(8,128)S(1)}, f32[8,256,256]{2,1,0:T(8,128)}, u32[]{:S(2)}) copy-start(f32[8,256,256]{2,1,0:T(8,128)} %online-softmax) | copy-start | bytes 6291460
  259.4 2.3 copy-start.5
  274.8 4.6 %copy-start.2 = (f32[8,256,256]{2,1,0:T(8,128)S(1)}, f32[8,256,256]{2,1,0:T(8,128)}, u32[]{:S(2)}) copy-start(f32[8,256,256]{2,1,0:T(8,128)} %online-softmax.1) | copy-start | bytes 6291460
  279.4 2.3 copy-start.4
  293.3 4.6 %copy-start = (f32[8,256,256]{2,1,0:T(8,128)S(1)}, f32[8,256,256]{2,1,0:T(8,128)}, u32[]{:S(2)}) copy-start(f32[8,256,256]{2,1,0:T(8,128)} %online-softmax.2) | copy-start | bytes 6291460
  297.9 2.3 copy-start.3
  300.2 2.2 copy-start.9
Sparse Core Ops, SparseCore 0:
  11.1 92.7 all-reduce.3
  146.3 90.7 all-reduce.5
where the time goes:
time: 321 us; the launch traced here: 320 us
  waiting for transfers between devices  147 us (46%)
  blocking collectives  62.9 us (20%)
  matrix products  55.3 us (17%)
  Pallas kernels  24.3 us (8%)
  between operations  13.7 us (4%)
  other arithmetic  10 us (3%)
  local copies, waits for them, and re-layouts  5.91 us (2%)
    psum x2, waiting for transfers between devices, shards(): q_sums, k_sums = lax.psum((q_part, k_part), ('seq', 'sub'))  147 us
    pmax x1, blocking collectives, shards(): row_top = lax.pmax(jnp.max(score_matrix, axis=2), ('seq', 'sub'))  32.4 us
    psum x1, blocking collectives, shards(): total, numer = lax.psum((total, numer), ('seq', 'sub'))  30.5 us
    unnamed x3, Pallas kernels  24.3 us
    dot_general x3, matrix products, iterative_pseudo_inverse(): jnp.einsum('hij,hjk->hik', product, 7.0 * identity - product, precision=H...  13.7 us
    dot_general x3, matrix products, iterative_pseudo_inverse(): jnp.einsum('hij,hjk->hik', iterate, 13.0 * identity - nested, precision=H...  10.7 us
    dot_general x3, matrix products, iterative_pseudo_inverse(): jnp.einsum('hij,hjk->hik', product, 15.0 * identity - nested, precision=H...  6.81 us
  transfers between devices with their start and end apart: 2, of which 2 were waited for; matrix products, arithmetic and copies ran while one was open for 2% of the time, Pallas kernels for 0%

commit v1 on v0

--- a/solution.py
+++ b/solution.py
@@ -90,7 +90,7 @@
         precision=HIGH_PRECISION,
         preferred_element_type=jnp.float32,
     )
-    total, numer = lax.psum((total, numer), ("seq", "sub"))
+    total, numer = lax.psum(lax.psum((total, numer), "sub"), "seq")
     landmark_values = numer / total[:, :, None]
     mixing_matrix = solve_mixing(query_head_rows, key_head_rows, landmark_values, score_scaling)
     scores_one = (

time: 321 us -> 300 us (0.935)
  blocking collectives: 62.9 us -> 49.4 us
  waiting for transfers between devices: 147 us -> 134 us
  matrix products: 55.3 us -> 61.5 us
    psum x2 -> x1, waiting for transfers between devices: 147 us -> 92.8 us  [shards(): q_sums, k_sums = lax.psum((q_part, k_part), ('seq', 'sub'))]
    psum x0 -> x2, waiting for transfers between devices: none -> 41.2 us  [shards(): total, numer = lax.psum(lax.psum((total, numer), 'sub'), 'seq')]
    psum x1 -> x2, blocking collectives: 30.5 us -> 18.3 us  [shards(): total, numer = lax.psum(lax.psum((total, numer), 'sub'), 'seq')]
  transfers between devices with their start and end apart: 2 -> 3, of which waited for: 2 -> 3; matrix products, arithmetic and copies ran while one was open for 2% -> 5% of each run, Pallas kernels for 0% -> 0%
where the time goes in v1:
time: 300 us; the launch traced here: 299 us
  waiting for transfers between devices  134 us (45%)
  matrix products  61.5 us (20%)
  blocking collectives  49.4 us (16%)
  Pallas kernels  24.4 us (8%)
  between operations  13.4 us (4%)
  other arithmetic  9.16 us (3%)
  local copies, waits for them, and re-layouts  7.52 us (3%)
    psum x1, waiting for transfers between devices, shards(): q_sums, k_sums = lax.psum((q_part, k_part), ('seq', 'sub'))  92.8 us
    psum x2, waiting for transfers between devices, shards(): total, numer = lax.psum(lax.psum((total, numer), 'sub'), 'seq')  41.2 us
    pmax x1, blocking collectives, shards(): row_top = lax.pmax(jnp.max(score_matrix, axis=2), ('seq', 'sub'))  31.1 us
    unnamed x3, Pallas kernels  24.4 us
    psum x2, blocking collectives, shards(): total, numer = lax.psum(lax.psum((total, numer), 'sub'), 'seq')  18.3 us
    dot_general x3, matrix products, iterative_pseudo_inverse(): jnp.einsum('hij,hjk->hik', product, 7.0 * identity - product, precision=H...  13.7 us
    dot_general x3, matrix products, iterative_pseudo_inverse(): jnp.einsum('hij,hjk->hik', iterate, 13.0 * identity - nested, precision=H...  13.7 us
    dot_general x3, matrix products, iterative_pseudo_inverse(): jnp.einsum('hij,hjk->hik', product, 15.0 * identity - nested, precision=H...  8.06 us
  transfers between devices with their start and end apart: 3, of which 3 were waited for; matrix products, arithmetic and copies ran while one was open for 5% of the time, Pallas kernels for 0%

profile of v1, /device:TPU:0, one launch (start us, length us, event | category | flops | bytes accessed | tf_op | source)
XLA Modules:
  0.0 299.4 jit_solution(11631899565975533977)
XLA Ops:
  8.6 2.4 fusion.58
  16.6 92.8 %all-reduce.9.cloned.1.call-done = (f32[256,512]{1,0:T(8,128)}, f32[256,512]{1,0:T(8,128)}) async-done(((f32[256,512]{1,0:T(8,128)}, f32[256,512]{1,0:T(8,128)}), (f32[256,512]{1,0:T(8,128)}, f32[256,512]{1,0:T(8,128)})) %all-reduce.9.cloned.1.call-update) | async-done | bytes 1048592 | tf_op jit(solution)/shard_map/psum | solution.py:68
  116.4 2.9 copy.29
  119.3 8.1 %online-softmax = f32[8,256,256]{2,1,0:T(8,128)} custom-call(f32[8,256,256]{2,1,0:T(8,128)} %convolution_multiply_fusion, f32[8,256,256]{2,1,0:T(8,128)} %copy.29), custom_call_target="tpu_custom_call" | custom-call | tf_op online-softmax
  127.4 4.6 %fusion.13 = f32[8,256,256]{2,1,0:T(8,128)S(1)} fusion(f32[8,256,256]{2,1,0:T(8,128)} %online-softmax, f32[256,256]{1,0:T(8,128)S(1)} %fusion.61), kind=kOutput, calls=%fused_computation.16 | convolution fusion | flops 1611137024 | bytes 4456448 | tf_op jit(solution)/shard_map/hij,hjk->hik/dot_general | solution.py:28
  134.3 5.0 %fusion.33 = f32[8,256,256]{2,1,0:T(8,128)} fusion(f32[8,256,256]{1,2,0:T(8,128)S(1)} %copy-done.5, f32[8,256,256]{2,1,0:T(8,128)S(1)} %fusion.30, f32[256,256]{1,0:T(8,128)S(1)} %fusion.63), kind=kOutput, calls=%fused_computation.39 | convolution fusion | flops 1611661312 | bytes 6553600 | tf_op jit(solution)/shard_map/hij,hjk->hik/dot_general | solution.py:34
  139.3 8.1 %online-softmax.1 = f32[8,256,256]{2,1,0:T(8,128)} custom-call(f32[8,256,256]{2,1,0:T(8,128)} %convolution_multiply_fusion, f32[8,256,256]{2,1,0:T(8,128)} %fusion.33), custom_call_target="tpu_custom_call" | custom-call | tf_op online-softmax
  147.4 4.6 %fusion.11 = f32[8,256,256]{2,1,0:T(8,128)S(1)} fusion(f32[8,256,256]{2,1,0:T(8,128)} %online-softmax.1, f32[256,256]{1,0:T(8,128)S(1)} %fusion.61), kind=kOutput, calls=%fused_computation.14 | convolution fusion | flops 1611137024 | bytes 4456448 | tf_op jit(solution)/shard_map/hij,hjk->hik/dot_general | solution.py:28
  154.3 3.6 %fusion.36 = f32[8,256,256]{2,1,0:T(8,128)} fusion(f32[8,256,256]{2,1,0:T(8,128)S(1)} %copy-done.4, f32[8,256,256]{2,1,0:T(8,128)S(1)} %fusion.26, f32[256,256]{1,0:T(8,128)S(1)} %fusion.63), kind=kOutput, calls=%fused_computation.40 | convolution fusion | flops 1611661312 | bytes 6553600 | tf_op jit(solution)/shard_map/hij,hjk->hik/dot_general | solution.py:34
  157.9 8.1 %online-softmax.2 = f32[8,256,256]{2,1,0:T(8,128)} custom-call(f32[8,256,256]{2,1,0:T(8,128)} %convolution_multiply_fusion, f32[8,256,256]{2,1,0:T(8,128)} %fusion.36), custom_call_target="tpu_custom_call" | custom-call | tf_op online-softmax
  166.0 4.6 %fusion.9 = f32[8,256,256]{2,1,0:T(8,128)S(1)} fusion(f32[8,256,256]{2,1,0:T(8,128)} %online-softmax.2, f32[256,256]{1,0:T(8,128)S(1)} %fusion.61), kind=kOutput, calls=%fused_computation.12 | convolution fusion | flops 1611137024 | bytes 4456448 | tf_op jit(solution)/shard_map/hij,hjk->hik/dot_general | solution.py:28
  170.6 3.5 %fusion.22 = f32[8,256,256]{2,1,0:T(8,128)} fusion(f32[8,256,256]{2,1,0:T(8,128)S(1)} %copy-done, f32[8,256,256]{2,1,0:T(8,128)S(1)} %fusion.9, f32[256,256]{1,0:T(8,128)S(1)} %fusion.62), kind=kOutput, calls=%fused_computation.26 | convolution fusion | flops 1611137024 | bytes 6553600 | tf_op jit(solution)/shard_map/hij,hjk->hik/dot_general | solution.py:31
  174.1 2.7 multiply_reduce_fusion
  176.9 31.1 %pmax.7 = f32[8,256]{1,0:T(8,128)S(1)} all-reduce(f32[8,256]{1,0:T(8,128)S(1)} %get-tuple-element.16), channel_id=1, replica_groups=mesh['doc'=2,'seq'=4,'sub'=4] {'seq','sub'}, use_global_device_ids=true, to_apply=%region_11.12 | all-reduce | flops 2048 | bytes 16384 | tf_op jit(solution)/shard_map/pmax | solution.py:83
  208.0 5.9 %fusion.6 = f32[8,256,64]{1,2,0:T(8,128)} fusion(bf16[512,8,64]{0,2,1:T(8,128)(2,1)S(1)} %bitcast.54, f32[8,256,512]{2,1,0:T(8,128)} %get-tuple-element.17, f32[8,256]{1,0:T(8,128)S(1)} %pmax.7), kind=kOutput, calls=%fused_computation.11 | convolution fusion | flops 807403520 | bytes 5251072 | tf_op jit(solution)/shard_map/ijv,vib->ijb/dot_general | solution.py:86
  213.9 3.4 %fusion.76 = (f32[512,8]{0,1:T(8,128)S(1)}, f32[512,8,256]{0,2,1:T(8,128)}) fusion(bf16[256,8,64]{0,2,1:T(8,128)(2,1)S(1)} %bitcast.53, bf16[512,8,64]{0,2,1:T(8,128)(2,1)S(1)} %bitcast.56), kind=kOutput, calls=%fused_computation.83 | convolution fusion | flops 137363712 | bytes 4997120 | tf_op jit(solution)/shard_map/sub | solution.py:16
  217.3 27.1 %all-reduce.5.cloned.1.call-done = f32[8,256,64]{1,2,0:T(8,128)} async-done(((f32[8,256,64]{1,2,0:T(8,128)}), f32[8,256,64]{1,2,0:T(8,128)}) %all-reduce.5.cloned.1.call-update) | async-done | bytes 524304 | tf_op jit(solution)/shard_map/psum | solution.py:93
  244.5 3.3 %fusion.5 = f32[8,256]{1,0:T(8,128)S(1)} fusion(f32[8,256,512]{2,1,0:T(8,128)} %get-tuple-element.17, f32[8,256]{1,0:T(8,128)S(1)} %pmax.7), kind=kLoop, calls=%fused_computation.10 | loop fusion | flops 3143680 | bytes 4210688 | tf_op jit(solution)/shard_map/reduce_sum | solution.py:85
  247.8 5.9 %psum.46 = f32[8,256]{1,0:T(8,128)S(1)} all-reduce(f32[8,256]{1,0:T(8,128)S(1)} %fusion.5), channel_id=1, replica_groups=mesh['doc'=2,'seq'=4,'sub'=4] {'sub'}, use_global_device_ids=true, to_apply=%region_15.16 | all-reduce | flops 2048 | bytes 16384 | tf_op jit(solution)/shard_map/psum | solution.py:93
  253.6 12.5 %psum.47 = f32[8,256]{1,0:T(8,128)S(1)} all-reduce(f32[8,256]{1,0:T(8,128)S(1)} %psum.46), channel_id=1, replica_groups=mesh['doc'=2,'seq'=4,'sub'=4] {'seq'}, use_global_device_ids=true, to_apply=%region_16.17 | all-reduce | flops 2048 | bytes 16384 | tf_op jit(solution)/shard_map/psum | solution.py:93
  266.1 5.1 %fusion.20 = f32[8,256,256]{2,1,0:T(8,128)} fusion(f32[8,256,256]{2,1,0:T(8,128)S(1)} %copy-done.3, f32[8,256,256]{2,1,0:T(8,128)} %fusion.22, f32[256,256]{1,0:T(8,128)S(1)} %fusion.63), kind=kOutput, calls=%fused_computation.24 | convolution fusion | flops 1611137024 | bytes 6553600 | tf_op jit(solution)/shard_map/hij,hjk->hik/dot_general | solution.py:34
  271.2 14.1 %all-reduce.7.cloned.1.call-done = f32[8,256,64]{1,2,0:T(8,128)} async-done(((f32[8,256,64]{1,2,0:T(8,128)}), f32[8,256,64]{1,2,0:T(8,128)}) %all-reduce.7.cloned.1.call-update) | async-done | bytes 524304 | tf_op jit(solution)/shard_map/psum | solution.py:93
  285.3 3.9 %fusion.40 = bf16[8,256,64]{1,2,0:T(8,128)(2,1)S(1)} fusion(f32[8,256,256]{2,1,0:T(8,128)} %fusion.20, f32[8,256,64]{1,2,0:T(8,128)} %all-reduce.7.cloned.1.call-done, f32[8,256]{1,0:T(8,128)S(1)} %psum.47), kind=kOutput, calls=%fused_computation.43 | convolution fusion | flops 403439616 | bytes 2891776 | tf_op jit(solution)/shard_map/gux,gxr->gur/dot_general | solution.py:48
  289.1 2.7 fusion.39
  (56 shorter events, 20.3 us)
Async XLA Ops:
  6.5 6.9 %copy-start.8 = (bf16[512,512]{1,0:T(8,128)(2,1)S(1)}, bf16[512,512]{1,0:T(8,128)(2,1)}, u32[]{:S(2)}) copy-start(bf16[512,512]{1,0:T(8,128)(2,1)} %param.5) | copy-start | bytes 1572868
  6.5 102.8 %all-reduce.9.cloned.1.call-start = ((), (), s32[]{:S(2)}) async-start(), calls=%async_computation.2 | async-start | bytes 2097152 | tf_op jit(solution)/shard_map/psum | solution.py:68
  8.6 5.8 %copy-start.9 = (bf16[512,512]{1,0:T(8,128)(2,1)S(1)}, bf16[512,512]{1,0:T(8,128)(2,1)}, u32[]{:S(2)}) copy-start(bf16[512,512]{1,0:T(8,128)(2,1)} %param.4) | copy-start | bytes 1572868
  11.0 4.5 %copy-start.10 = (bf16[512,512]{1,0:T(8,128)(2,1)S(1)}, bf16[512,512]{1,0:T(8,128)(2,1)}, u32[]{:S(2)}) copy-start(bf16[512,512]{1,0:T(8,128)(2,1)} %param.6) | copy-start | bytes 1572868
  13.3 231.1 %all-reduce.5.cloned.1.call-start = ((), (), s32[]{:S(2)}) async-start(), calls=%async_computation | async-start | bytes 1048576 | tf_op jit(solution)/shard_map/psum | solution.py:93
  127.4 4.6 %copy-start.1 = (f32[8,256,256]{2,1,0:T(8,128)S(1)}, f32[8,256,256]{2,1,0:T(8,128)}, u32[]{:S(2)}) copy-start(f32[8,256,256]{2,1,0:T(8,128)} %online-softmax) | copy-start | bytes 6291460
  132.0 2.3 copy-start.5
  147.4 4.6 %copy-start.2 = (f32[8,256,256]{2,1,0:T(8,128)S(1)}, f32[8,256,256]{2,1,0:T(8,128)}, u32[]{:S(2)}) copy-start(f32[8,256,256]{2,1,0:T(8,128)} %online-softmax.1) | copy-start | bytes 6291460
  152.0 2.3 copy-start.4
  166.0 4.6 %copy-start = (f32[8,256,256]{2,1,0:T(8,128)S(1)}, f32[8,256,256]{2,1,0:T(8,128)}, u32[]{:S(2)}) copy-start(f32[8,256,256]{2,1,0:T(8,128)} %online-softmax.2) | copy-start | bytes 6291460
  170.6 3.5 %copy-start.7 = (bf16[512,512]{0,1:T(8,128)(2,1)S(1)}, bf16[512,512]{0,1:T(8,128)(2,1)}, u32[]{:S(2)}) copy-start(bf16[512,512]{0,1:T(8,128)(2,1)} %copy.31) | copy-start | bytes 1572868
  174.1 33.8 %copy-start.6 = (bf16[512,512]{0,1:T(8,128)(2,1)S(1)}, bf16[512,512]{0,1:T(8,128)(2,1)}, u32[]{:S(2)}) copy-start(bf16[512,512]{0,1:T(8,128)(2,1)} %copy.32) | copy-start | bytes 1572868
  208.0 5.9 %copy-start.11 = (bf16[512,512]{0,1:T(8,128)(2,1)S(1)}, bf16[512,512]{0,1:T(8,128)(2,1)}, u32[]{:S(2)}) copy-start(bf16[512,512]{0,1:T(8,128)(2,1)} %copy.33) | copy-start | bytes 1572868
  213.9 71.4 %all-reduce.7.cloned.1.call-start = ((), (), s32[]{:S(2)}) async-start(), calls=%async_computation.1 | async-start | bytes 1048576 | tf_op jit(solution)/shard_map/psum | solution.py:93
  244.5 21.6 %copy-start.3 = (f32[8,256,256]{2,1,0:T(8,128)S(1)}, f32[8,256,256]{2,1,0:T(8,128)}, u32[]{:S(2)}) copy-start(f32[8,256,256]{2,1,0:T(8,128)} %fusion.36) | copy-start | bytes 6291460
Sparse Core Ops, SparseCore 0:
  13.5 95.8 all-reduce.8
  214.0 30.3 all-reduce.4
  246.8 38.4 all-reduce.6
